TPU v7x, 512 devices: a whole 4x4x16 slice. The times are simulated.
512 devices in a mesh: row: 32 (over z, core), col: 16 (over x, y).
Axes of the slice: x: 4, y: 4, z: 16, core: 2. Of those that a mesh axis runs over, the one named last changes fastest.
Arguments:
- tiles: float32 [4096, 128, 128], P(('row', 'col')), may hold values from -0.48 to 0.48
- tile_rows: int32 [4096], P(('row', 'col')), may hold values from 0 to 255, as said below
- tile_cols: int32 [4096], P(('row', 'col')), may hold values from 0 to 511
- tile_count: int32 [512], P(('row', 'col')), may hold values from 1 to 8, as said below
- energy: float32 [1048576], P(('row', 'col')), may hold values from 0.4 to 10
- basis_block: float32 [4, 1048576], P(None, ('row', 'col')), may hold values from -14 to 14
- previous_block: float32 [4, 1048576], P(None, ('row', 'col')), may hold values from -6 to 6
- coupling: float32 [4, 4], replicated, may hold values from -2.5 to 2.5
Outputs:
- next_block: float32 [4, 1048576], P(None, ('row', 'col'))
- alpha: float32 [4, 4], replicated
- beta: float32 [4, 4], replicated
Inputs may be any that keep to these rules, and one draw needn't show every extreme that they name: `tile_rows`: every placed tile lies on or above the tile diagonal of the 1048576 x 1048576 matrix; slots may place the same tile more than once, and their tiles add. `tile_count`: the first device holds 8 live slots.
All inputs are finite; a program needn't handle non-finite values.
Results may differ from a plain program's by a relative error of at most 0.0003.
Values sent between devices are 32-bit elements; how exact they have to be, the bound alone decides.
A program may use at most 128 MiB of HBM per device.

v0:
```python
import jax
import jax.numpy as jnp
from jax import lax
from jax.sharding import PartitionSpec as P

TILE = 128


HIGH = lax.Precision.HIGHEST


def body(tiles, tile_rows, tile_cols, tile_count, energy, basis_block, previous_block, coupling):
    vectors = basis_block.shape[0]
    width = basis_block.shape[1]
    slots = tiles.shape[0]
    total = float(width * lax.axis_size("row") * lax.axis_size("col"))
    row_vec = lax.all_gather(basis_block, "col", axis=1, tiled=True)
    col_vec = lax.all_gather(basis_block, "row", axis=1, tiled=True)
    live = (jnp.arange(slots, dtype=jnp.int32) < tile_count[0]).astype(jnp.float32)
    row_tiles = row_vec.shape[1] // TILE
    col_tiles = col_vec.shape[1] // TILE
    x_cols = jnp.take(col_vec.reshape(vectors, col_tiles, TILE), tile_cols, axis=1)
    x_rows = jnp.take(row_vec.reshape(vectors, row_tiles, TILE), tile_rows, axis=1)
    direct = jnp.einsum("kmj,mij->kmi", x_cols, tiles, precision=HIGH) * live[None, :, None]
    flipped = jnp.einsum("kmi,mij->kmj", x_rows, tiles, precision=HIGH) * live[None, :, None]
    hot_rows = (tile_rows[:, None] == jnp.arange(row_tiles, dtype=jnp.int32)[None, :]).astype(
        jnp.float32
    )
    hot_cols = (tile_cols[:, None] == jnp.arange(col_tiles, dtype=jnp.int32)[None, :]).astype(
        jnp.float32
    )
    row_part = jnp.einsum("kmi,mr->kri", direct, hot_rows, precision=HIGH).reshape(
        vectors, row_tiles * TILE
    )
    col_part = jnp.einsum("kmj,mc->kcj", flipped, hot_cols, precision=HIGH).reshape(
        vectors, col_tiles * TILE
    )
    row_total = lax.psum_scatter(row_part, "col", scatter_dimension=1, tiled=True)
    col_total = lax.psum_scatter(col_part, "row", scatter_dimension=1, tiled=True)
    image = row_total + col_total + energy[None, :] * basis_block
    residual0 = image - jnp.dot(coupling, previous_block, precision=HIGH)
    first = lax.psum(jnp.dot(basis_block, residual0.T, precision=HIGH), ("row", "col")) / total
    residual1 = residual0 - jnp.dot(first.T, basis_block, precision=HIGH)
    second = lax.psum(jnp.dot(basis_block, residual1.T, precision=HIGH), ("row", "col")) / total
    residual2 = residual1 - jnp.dot(second.T, basis_block, precision=HIGH)
    alpha = first + second
    gram = lax.psum(jnp.dot(residual2, residual2.T, precision=HIGH), ("row", "col")) / total
    lower = jnp.linalg.cholesky(gram)
    next_block = lax.linalg.triangular_solve(lower, residual2, left_side=True, lower=True)
    return (next_block, alpha, lower.T)


def solution(mesh):
    return jax.shard_map(
        body,
        mesh=mesh,
        in_specs=(
            P(("row", "col"), None, None),
            P(("row", "col")),
            P(("row", "col")),
            P(("row", "col")),
            P(("row", "col")),
            P(None, ("row", "col")),
            P(None, ("row", "col")),
            P(),
        ),
        out_specs=(P(None, ("row", "col")), P(), P()),
        check_vma=False,
    )
```

profile of v0, /device:TPU:1, one launch (start us, length us, event | category | flops | bytes accessed | tf_op | source)
XLA Modules:
  0.0 728.1 jit_solution(8581407686291507893)
XLA Ops:
  7.2 0.7 all-gather.2.cloned.1.call-update
  8.6 0.7 compare_select_fusion
  9.3 20.0 %all_gather.7 = f32[4,32768]{1,0:T(4,128)S(1)} all-gather(f32[4,2048]{1,0:T(4,128)} %param.13), channel_id=1, replica_groups=mesh['row'=32,'col'=16] {'col'}, dimensions={1}, use_global_device_ids=true | all-gather | bytes 557056 | tf_op jit(solution)/shard_map/all_gather | solution.py:17
  29.2 0.6 gather_fusion.1
  29.8 0.7 compare_and_fusion
  30.5 0.6 fusion
  31.1 1.4 convolution_bitcast_fusion
  32.5 15.9 %copy.34 = f32[4,512,128]{0,2,1:T(8,128)} copy(f32[4,512,128]{2,1,0:T(8,128)S(1)} %convolution_bitcast_fusion) | data formatting | bytes 2097152
  48.5 38.1 %all-gather.2.cloned.1.call-done = f32[4,65536]{1,0:T(4,128)} async-done(((f32[4,2048]{1,0:T(4,128)}), f32[4,65536]{1,0:T(4,128)}) %all-gather.2.cloned.1.call-update) | async-done | bytes 1048592 | tf_op jit(solution)/shard_map/all_gather | solution.py:18
  86.5 1.8 gather_fusion
  88.3 1.0 fusion.1
  89.8 8.6 %copy.33 = f32[4,256,128]{0,2,1:T(8,128)} copy(f32[4,256,128]{2,1,0:T(8,128)S(1)} %convolution_bitcast_fusion.1) | data formatting | bytes 1048576
  98.4 182.2 %reduce-scatter.9.cloned.1.call-done = f32[2048,4]{1,0:T(8,128)} async-done(((f32[65536,4]{1,0:T(8,128)}), f32[2048,4]{1,0:T(8,128)}) %reduce-scatter.9.cloned.1.call-update) | async-done | bytes 32784
  280.6 1.6 copy.32
  282.2 128.0 %reduce-scatter.7.cloned.1.call-done = f32[2048,4]{1,0:T(8,128)} async-done(((f32[32768,4]{1,0:T(8,128)}), f32[2048,4]{1,0:T(8,128)}) %reduce-scatter.7.cloned.1.call-update) | async-done | bytes 32784
  410.2 1.6 copy.30
  412.2 104.5 %psum.21 = f32[4,4]{0,1:T(4,128)S(1)} all-reduce(f32[4,4]{0,1:T(4,128)S(1)} %convolution_bitcast_fusion.3), channel_id=1, replica_groups=mesh['row'=32,'col'=16] {'row','col'}, use_global_device_ids=true, to_apply=%region_2.3 | all-reduce | flops 16 | bytes 128 | tf_op jit(solution)/shard_map/psum | solution.py:42
  517.0 100.4 %psum.22 = f32[4,4]{0,1:T(4,128)S(1)} all-reduce(f32[4,4]{0,1:T(4,128)S(1)} %convolution_bitcast_fusion.2), channel_id=1, replica_groups=mesh['row'=32,'col'=16] {'row','col'}, use_global_device_ids=true, to_apply=%region_3.4 | all-reduce | flops 16 | bytes 128 | tf_op jit(solution)/shard_map/psum | solution.py:44
  617.8 99.4 %psum.23 = f32[4,4]{0,1:T(4,128)S(1)} all-reduce(f32[4,4]{0,1:T(4,128)S(1)} %fusion.30), channel_id=1, replica_groups=mesh['row'=32,'col'=16] {'row','col'}, use_global_device_ids=true, to_apply=%region_4.5 | all-reduce | flops 16 | bytes 128 | tf_op jit(solution)/shard_map/psum | solution.py:47
  717.8 0.6 compare_reduce_fusion
  718.4 0.6 fusion.23
  719.4 0.9 fusion.18
  720.3 0.7 copy.27
  721.0 0.7 copy.26
  (38 shorter events, 2.7 us)
Async XLA Ops:
  7.2 23.3 %copy-start = (f32[8,128,128]{2,1,0:T(8,128)S(1)}, f32[8,128,128]{2,1,0:T(8,128)}, u32[]{:S(2)}) copy-start(f32[8,128,128]{2,1,0:T(8,128)} %param.8) | copy-start | bytes 1572868
  7.2 79.4 %all-gather.2.cloned.1.call-start = ((), (), s32[]{:S(2)}) async-start(), calls=%async_computation.2 | async-start | bytes 1081344 | tf_op jit(solution)/shard_map/all_gather | solution.py:18
  7.9 272.7 %reduce-scatter.9.cloned.1.call-start = ((), (), s32[]{:S(2)}) async-start(), calls=%async_computation.4 | async-start | bytes 34603008
  32.4 16.0 %copy-start.5 = (s32[8]{0:T(128)S(1)}, s32[8]{0:T(128)}, u32[]{:S(2)}) copy-start(s32[8]{0:T(128)} %param.10) | copy-start | bytes 100
  32.4 56.9 %copy-start.6 = (s32[8]{0:T(128)S(1)}, s32[8]{0:T(128)}, u32[]{:S(2)}) copy-start(s32[8]{0:T(128)} %param.9) | copy-start | bytes 100
  48.3 363.4 %copy-start.1 = (f32[4,2048]{1,0:T(4,128)S(1)}, f32[4,2048]{1,0:T(4,128)}, u32[]{:S(2)}) copy-start(f32[4,2048]{1,0:T(4,128)} %param.13) | copy-start | bytes 98308
  48.3 363.4 %copy-start.2 = (f32[4,2048]{1,0:T(4,128)S(1)}, f32[4,2048]{1,0:T(4,128)}, u32[]{:S(2)}) copy-start(f32[4,2048]{1,0:T(4,128)} %param.14) | copy-start | bytes 98308
  48.3 363.4 %copy-start.3 = (f32[2048]{0:T(1024)S(1)}, f32[2048]{0:T(1024)}, u32[]{:S(2)}) copy-start(f32[2048]{0:T(1024)} %param.12) | copy-start | bytes 24580
  48.3 363.4 %copy-start.4 = (f32[4,4]{1,0:T(4,128)S(1)}, f32[4,4]{1,0:T(4,128)}, u32[]{:S(2)}) copy-start(f32[4,4]{1,0:T(4,128)} %param.15) | copy-start | bytes 196
  48.4 361.8 %reduce-scatter.7.cloned.1.call-start = ((), (), s32[]{:S(2)}) async-start(), calls=%async_computation.3 | async-start | bytes 17825792
Sparse Core Ops, SparseCore 0:
  10.1 76.3 all-gather.1
  89.4 191.1 reduce-scatter.8
  284.9 125.2 reduce-scatter.6
where the time goes:
time: 729 us; the launch traced here: 728 us
  waiting for transfers between devices  349 us (48%)
  blocking collectives  324 us (44%)
  local copies, waits for them, and re-layouts  31.4 us (4%)
  between operations  14.5 us (2%)
    unnamed x5, waiting for transfers between devices  311 us
    psum x1, blocking collectives, body(): lax.psum(jnp.dot(basis_block, residual0.T, precision=HIGH), ('row', 'col'))  104 us
    psum x1, blocking collectives, body(): lax.psum(jnp.dot(basis_block, residual1.T, precision=HIGH), ('row', 'col'))  100 us
    psum x1, blocking collectives, body(): lax.psum(jnp.dot(residual2, residual2.T, precision=HIGH), ('row', 'col'))  99.4 us
    all_gather x1, waiting for transfers between devices, body(): col_vec = lax.all_gather(basis_block, 'row', axis=1, tiled=True)  38.1 us
    unnamed x20, local copies, waits for them, and re-layouts  28.9 us
    all_gather x1, blocking collectives, body(): row_vec = lax.all_gather(basis_block, 'col', axis=1, tiled=True)  20 us
  transfers between devices with their start and end apart: 3, of which 3 were waited for; matrix products, arithmetic and copies ran while one was open for 5% of the time, Pallas kernels for 0%

commit v1 on v0

v1 whole, which is shorter than its diff:
```python
import jax
import jax.numpy as jnp
from jax import lax
from jax.experimental import pallas as pl
from jax.experimental.pallas import tpu as pltpu
from jax.sharding import PartitionSpec as P

MESH = pl.DeviceIdType.MESH
HIGH = lax.Precision.HIGHEST
F32 = jnp.float32
ROWS, COLS, CHIPS = 32, 16, 16
K, SLOTS, TILE, WIDTH = 4, 8, 128, 2048
BLOCKS = WIDTH // TILE
CHUNK = BLOCKS + 1
TOTAL = float(WIDTH * ROWS * COLS)
REACH = {1: CHIPS // 2, -1: CHIPS // 2 - 1}
HOP = 2


def dot(a, b, trans_b=False):
    dims = (((1,), (1 if trans_b else 0,)), ((), ()))
    return lax.dot_general(a, b, dims, precision=HIGH, preferred_element_type=F32)


def two_sum(a, b):
    s = a + b
    t = s - a
    return s, (a - (s - t)) + (b - t)


def split(a):
    c = a * 4097.0
    high = c - (c - a)
    return high, a - high


def two_prod(a, b):
    p = a * b
    ah, al = split(a)
    bh, bl = split(b)
    return p, ((ah * bh - p) + ah * bl + al * bh) + al * bl


def fold_rows(x, e):
    for s in (4, 2, 1):
        x, r = two_sum(x, pltpu.roll(x, s, 0))
        e = e + pltpu.roll(e, s, 0) + r
    return x, e


def sum_pairs(rows):
    x, e = rows[0:8], jnp.zeros((8, TILE), F32)
    for r in range(8, rows.shape[0], 8):
        x, t = two_sum(x, rows[r : r + 8])
        e = e + t
    x, e = fold_rows(x, e)
    lane = lax.broadcasted_iota(jnp.int32, (8, TILE), 1)
    return x + jnp.where(lane >= 64, pltpu.roll(e, 64, 1), 0.0)


def pick(row, base, stride_m, stride_k, stride_l, shift=0):
    src = lax.broadcasted_iota(jnp.int32, (TILE, TILE), 0)
    lane = lax.broadcasted_iota(jnp.int32, (TILE, TILE), 1)
    m, k, l = lane // 16, (lane // 4) % 4, lane % 4
    want = base + shift + stride_m * m + stride_k * k + stride_l * l
    hot = jnp.where((src == want) & (lane < 64), 1.0, 0.0).astype(F32)
    return dot(row, hot)


def fold_m(x, e):
    for s in (32, 16):
        x, r = two_sum(x, pltpu.roll(x, TILE - s, 1))
        e = e + pltpu.roll(e, TILE - s, 1) + r
    return x, e


def body(rows, cols, count, coupling, tiles_hbm, energy_hbm, basis_hbm, prev_hbm,
         next_ref, alpha_ref, beta_ref,
         xcol, xrow, tiles, energy, prev, fsend, fbuf, dsend, dbuf, gather, red1, red2, msg,
         local, xs, xr, hs, hr, ps, pr, fs, fr, gs, gr, ds, dr, as1, ar1, as2, ar2):
    i, j = lax.axis_index("row"), lax.axis_index("col")
    sib = (i + 1 - 2 * lax.rem(i, 2), j)

    def chip(d):
        return (lax.rem(i + 2 * d + ROWS, ROWS), j)

    def plane(d):
        return (i, lax.rem(j + d, COLS))

    def send(src, dst, s, r, dev):
        c = pltpu.make_async_remote_copy(
            src_ref=src, dst_ref=dst, send_sem=s, recv_sem=r, device_id=dev, device_id_type=MESH
        )
        c.start()
        return c

    loads = [
        pltpu.make_async_copy(basis_hbm, xcol.at[pl.ds(i * CHUNK, BLOCKS)], local.at[0]),
        pltpu.make_async_copy(basis_hbm, xrow.at[pl.ds(j * CHUNK, BLOCKS)], local.at[1]),
        pltpu.make_async_copy(tiles_hbm, tiles, local.at[2]),
        pltpu.make_async_copy(energy_hbm, energy, local.at[3]),
        pltpu.make_async_copy(prev_hbm, prev, local.at[4]),
    ]
    for c in loads:
        c.start()

    barrier = pltpu.get_barrier_semaphore()
    near = [chip(s * d) for d in range(1, HOP + 1) for s in (1, -1)] + [sib]
    for dev in near:
        pl.semaphore_signal(barrier, inc=1, device_id=dev, device_id_type=MESH)

    @pl.loop(1, COLS)
    def _(d):
        pl.semaphore_signal(barrier, inc=1, device_id=plane(d), device_id_type=MESH)

    sub = lax.broadcasted_iota(jnp.int32, (K, TILE), 0)
    lane = lax.broadcasted_iota(jnp.int32, (K, TILE), 1)
    places = jnp.zeros((K, TILE), F32)
    for t in range(SLOTS):
        live = jnp.full((K, TILE), t, jnp.int32) < jnp.full((K, TILE), count[0], jnp.int32)
        c = jnp.where(live, jnp.full((K, TILE), cols[t], jnp.int32), -1).astype(F32)
        r = jnp.where(live, jnp.full((K, TILE), rows[t], jnp.int32), -1).astype(F32)
        places = jnp.where((sub == i // 16) & (lane == lax.rem(i, 16) * SLOTS + t), c, places)
        places = jnp.where((sub == 2) & (lane == j * SLOTS + t), r, places)
    xcol[i * CHUNK + BLOCKS] = places
    xrow[j * CHUNK + BLOCKS] = places
    loads[0].wait()
    loads[1].wait()
    pl.semaphore_wait(barrier, len(near) + COLS - 1)

    def place(buf, slot):
        return buf.at[pl.ds(slot * CHUNK, CHUNK)] if buf is xcol or buf is xrow else buf.at[slot]

    def ring(buf, ssem, rsem, copies, base, s):
        at = place(buf, lax.rem(i - 2 * s * base + 2 * ROWS, ROWS))
        for d in range(HOP, 0, -1):
            t = base + d
            if t <= REACH[s]:
                n = 2 * (t - 1) + (s < 0)
                copies[(t, s)] = send(at, at, ssem.at[n], rsem.at[n], chip(s * d))

    def share(buf, ssem, rsem, copies, t, s):
        at = place(buf, lax.rem(i - 2 * s * t + 2 * ROWS, ROWS))
        n = len(copies)
        copies.append(send(at, at, ssem.at[n], rsem.at[n], sib))

    def arrive(buf, sems, ssems, copies, shares, hops):
        for t in hops:
            for s in (1, -1):
                if t <= REACH[s]:
                    copies[(t, s)].wait_recv()
                    if t % HOP == 0:
                        ring(buf, *sems, copies, t, s)
        for t in hops:
            for s in (1, -1):
                if t <= REACH[s]:
                    share(buf, *ssems, shares, t, s)

    def over_plane(src, dst, ssem, rsem):
        @pl.loop(1, COLS)
        def _(d):
            send(src, dst, ssem.at[d], rsem.at[d], plane(d))

    def plane_wait(src, dst, ssem, rsem):
        @pl.loop(1, COLS)
        def _(d):
            c = pltpu.make_async_remote_copy(
                src_ref=src, dst_ref=dst, send_sem=ssem.at[d], recv_sem=rsem.at[d],
                device_id=plane(d), device_id_type=MESH,
            )
            c.wait()

    xc, xh, fc, fh = {}, [], {}, []
    ring(xcol, xs, xr, xc, 0, 1)
    ring(xcol, xs, xr, xc, 0, -1)
    share(xcol, hs, hr, xh, 0, 1)
    own = place(xrow, j)
    over_plane(own, own, ps, pr)

    for c in loads[2:]:
        c.wait()

    arrive(xcol, (xs, xr), (hs, hr), xc, xh, (1, 2))
    plane_wait(own, own, ps, pr)

    for t in range(SLOTS):
        r = rows[t]
        v = xrow[r + lax.shift_right_logical(r, 4)]
        y = dot(v, tiles[t])
        for k in range(K):
            fsend[k, t : t + 1, :] = y[k : k + 1, :]
    fbuf[i] = fsend[...]
    ring(fbuf, fs, fr, fc, 0, 1)
    ring(fbuf, fs, fr, fc, 0, -1)
    share(fbuf, gs, gr, fh, 0, 1)

    arrive(xcol, (xs, xr), (hs, hr), xc, xh, (3, 4))
    arrive(fbuf, (fs, fr), (gs, gr), fc, fh, (1, 2))
    arrive(xcol, (xs, xr), (hs, hr), xc, xh, (5, 6))
    arrive(fbuf, (fs, fr), (gs, gr), fc, fh, (3, 4))
    arrive(xcol, (xs, xr), (hs, hr), xc, xh, (7, 8))
    for c in xh:
        c.wait()

    for t in range(SLOTS):
        r = cols[t]
        v = xcol[r + lax.shift_right_logical(r, 4)]
        y = dot(v, tiles[t], trans_b=True)
        for k in range(K):
            dsend[k, t : t + 1, :] = y[k : k + 1, :]
    dbuf[j] = dsend[...]
    over_plane(dbuf.at[j], dbuf.at[j], ds, dr)
    arrive(fbuf, (fs, fr), (gs, gr), fc, fh, (5, 6))

    at_cols = jnp.zeros((K, TILE), F32)
    for d in range(ROWS):
        at_cols = at_cols + xcol[d * CHUNK + BLOCKS]
    at_rows = jnp.zeros((K, TILE), F32)
    for d in range(COLS):
        at_rows = at_rows + xrow[d * CHUNK + BLOCKS]
    block = lax.broadcasted_iota(jnp.int32, (BLOCKS, TILE), 0)

    def hot(line, first):
        return jnp.where(line.astype(jnp.int32) == block + first * BLOCKS, 1.0, 0.0).astype(F32)

    hot_low = hot(at_cols[0:1, :], i)
    hot_high = hot(at_cols[1:2, :], i)
    hot_row = hot(at_rows[2:3, :], j)

    x = [xcol[pl.ds(i * CHUNK, BLOCKS), k, :] for k in range(K)]
    old = [prev[:, k, :] for k in range(K)]
    res = []
    for k in range(K):
        r = energy[...] * x[k]
        for m in range(K):
            r = r - coupling[k, m] * old[m]
        res.append(r)

    gather[...] = jnp.zeros((TILE, TILE), F32)

    def inner(row, a, b):
        gather[row : row + 1, :] = jnp.sum(a * b, axis=0, keepdims=True)

    for k in range(K):
        for l in range(K):
            inner(4 * k + l, x[k], x[l])

    arrive(fbuf, (fs, fr), (gs, gr), fc, fh, (7, 8))
    for c in fh:
        c.wait()
    for k in range(K):
        low = fbuf[0:16, k].reshape(TILE, TILE)
        high = fbuf[16:32, k].reshape(TILE, TILE)
        res[k] = res[k] + (dot(hot_low, low) + dot(hot_high, high))
    plane_wait(dbuf.at[j], dbuf.at[j], ds, dr)
    for k in range(K):
        res[k] = res[k] + dot(hot_row, dbuf[:, k].reshape(TILE, TILE))

    for k in range(K):
        for l in range(K):
            inner(16 + 4 * k + l, x[k], res[l])
            inner(32 + 4 * k + l, res[k], res[l])
    here = dot(jnp.ones((8, TILE), F32), gather[...], trans_b=True)

    msg[0] = here[0:1]
    red1[j] = here[0:1]

    over_plane(msg.at[0], red1.at[j], as1, ar1)
    plane_wait(msg.at[0], red1.at[j], as1, ar1)
    part = sum_pairs(red1[...].reshape(COLS, TILE))
    msg[1] = part[0:1]
    red2[i] = part[0:1]

    def column(d):
        return pltpu.make_async_remote_copy(
            src_ref=msg.at[1], dst_ref=red2.at[i], send_sem=as2.at[d], recv_sem=ar2.at[d],
            device_id=(lax.rem(i + d, ROWS), j), device_id_type=MESH,
        )

    @pl.loop(1, ROWS)
    def _(d):
        column(d).start()

    @pl.loop(1, ROWS)
    def _(d):
        column(d).wait()

    sums = sum_pairs(red2[...].reshape(ROWS, TILE)) * (1.0 / TOTAL)

    g_km, g_km_low = pick(sums, 0, 1, 4, 0), pick(sums, 0, 1, 4, 0, 64)
    f_ml = pick(sums, 16, 4, 0, 1)
    f_mk, f_mk_low = pick(sums, 16, 4, 1, 0), pick(sums, 16, 4, 1, 0, 64)
    first = pltpu.roll(sums, TILE - 16, 1)
    gf, _ = fold_m(g_km * f_ml, jnp.zeros_like(g_km))
    alpha = first + (first - gf)
    a_ml, a_mk = pick(alpha, 0, 4, 0, 1), pick(alpha, 0, 4, 1, 0)
    p, e = two_prod(g_km, a_ml)
    p, e = fold_m(p, e + g_km_low * a_ml)
    p, r = two_sum(p, -first)
    e = e + r - pltpu.roll(sums, TILE - 80, 1)
    p, e = two_sum(p, e)
    t_ml, t_ml_low = pick(p, 0, 4, 0, 1), pick(e, 0, 4, 0, 1)
    p, e = two_prod(a_mk, t_ml)
    q, r = two_prod(-f_mk, a_ml)
    p, s = two_sum(p, q)
    p, e = fold_m(p, e + r + s + a_mk * t_ml_low - f_mk_low * a_ml)
    p, r = two_sum(p, pltpu.roll(sums, TILE - 32, 1))
    gram = p + (e + r + pltpu.roll(sums, TILE - 96, 1))

    def entry(v, k, l):
        return v[0:1, 4 * k + l : 4 * k + l + 1]

    low = {}
    inv = []
    for k in range(K):
        d = entry(gram, k, k)
        for m in range(k):
            d = d - low[k, m] * low[k, m]
        low[k, k] = jnp.sqrt(d)
        inv.append(1.0 / low[k, k])
        for n in range(k + 1, K):
            v = entry(gram, n, k)
            for m in range(k):
                v = v - low[n, m] * low[k, m]
            low[n, k] = v * inv[k]

    done = []
    for l in range(K):
        r = res[l]
        for k in range(K):
            r = r - entry(alpha, k, l) * x[k]
        for m in range(l):
            r = r - low[l, m] * done[m]
        done.append(r * inv[l])
    for k in range(K):
        next_ref[:, k, :] = done[k]

    row4 = lax.broadcasted_iota(jnp.int32, (K, K), 0)
    col4 = lax.broadcasted_iota(jnp.int32, (K, K), 1)
    a, b = jnp.zeros((K, K), F32), jnp.zeros((K, K), F32)
    for k in range(K):
        for l in range(K):
            a = jnp.where((row4 == k) & (col4 == l), entry(alpha, k, l), a)
            if l >= k:
                b = jnp.where((row4 == k) & (col4 == l), low[l, k], b)
    alpha_ref[...] = a
    beta_ref[...] = b

    for c in list(xc.values()) + list(fc.values()):
        c.wait_send()


def step(tiles, tile_rows, tile_cols, tile_count, energy, basis_block, previous_block, coupling):
    vmem, smem, hbm = (pl.BlockSpec(memory_space=m) for m in (pltpu.VMEM, pltpu.SMEM, pl.ANY))
    dma = pltpu.SemaphoreType.DMA
    def blocked(a):
        return a.reshape(K, BLOCKS, TILE).transpose(1, 0, 2)

    out, alpha, beta = pl.pallas_call(
        body,
        out_shape=(
            jax.ShapeDtypeStruct((BLOCKS, K, TILE), F32),
            jax.ShapeDtypeStruct((K, K), F32),
            jax.ShapeDtypeStruct((K, K), F32),
        ),
        in_specs=[smem] * 4 + [hbm] * 4,
        out_specs=(vmem, vmem, vmem),
        scratch_shapes=[
            pltpu.VMEM((ROWS * CHUNK, K, TILE), F32),
            pltpu.VMEM((COLS * CHUNK, K, TILE), F32),
            pltpu.VMEM((SLOTS, TILE, TILE), F32),
            pltpu.VMEM((BLOCKS, TILE), F32),
            pltpu.VMEM((BLOCKS, K, TILE), F32),
            pltpu.VMEM((K, SLOTS, TILE), F32),
            pltpu.VMEM((ROWS, K, SLOTS, TILE), F32),
            pltpu.VMEM((K, SLOTS, TILE), F32),
            pltpu.VMEM((COLS, K, SLOTS, TILE), F32),
            pltpu.VMEM((TILE, TILE), F32),
            pltpu.VMEM((COLS, 1, TILE), F32),
            pltpu.VMEM((ROWS, 1, TILE), F32),
            pltpu.VMEM((2, 1, TILE), F32),
            dma((5,)),
            dma((CHIPS,)), dma((CHIPS,)), dma((CHIPS,)), dma((CHIPS,)),
            dma((COLS,)), dma((COLS,)),
            dma((CHIPS,)), dma((CHIPS,)), dma((CHIPS,)), dma((CHIPS,)),
            dma((COLS,)), dma((COLS,)),
            dma((COLS,)), dma((COLS,)),
            dma((ROWS,)), dma((ROWS,)),
        ],
        compiler_params=pltpu.CompilerParams(
            collective_id=0, has_side_effects=True, vmem_limit_bytes=56 << 20
        ),
        name="lanczos",
    )(
        tile_rows, tile_cols, tile_count, coupling, tiles, energy.reshape(BLOCKS, TILE),
        blocked(basis_block), blocked(previous_block),
    )
    return out.transpose(1, 0, 2).reshape(K, WIDTH), alpha, beta


def solution(mesh):
    both = ("row", "col")
    return jax.shard_map(
        step,
        mesh=mesh,
        in_specs=(
            P(both, None, None), P(both), P(both), P(both), P(both), P(None, both), P(None, both), P(),
        ),
        out_specs=(P(None, both), P(), P()),
        check_vma=False,
    )
```

time: 729 us -> 66.4 us (0.09)
  waiting for transfers between devices: 349 us -> 0 us
  blocking collectives: 324 us -> 0 us
  Pallas kernels: 0 us -> 62.2 us
  local copies, waits for them, and re-layouts: 31.4 us -> 2.64 us
  between operations: 14.5 us -> 1.3 us
    unnamed x5 -> x0, waiting for transfers between devices: 311 us -> none
    psum x3 -> x0, blocking collectives: 304 us -> none  [the longest x1 104 us: body(): lax.psum(jnp.dot(basis_block, residual0.T, precision=HIGH), ('row', 'col'))]
    pallas_call x0 -> x1, Pallas kernels: none -> 62.2 us  [step(): pl.pallas_call(body, out_shape=(jax.ShapeDtypeStruct((BLOCKS, K, TILE), F...]
    all_gather x1 -> x0, waiting for transfers between devices: 38.1 us -> none  [body(): col_vec = lax.all_gather(basis_block, 'row', axis=1, tiled=True)]
    unnamed x20 -> x7, local copies, waits for them, and re-layouts: 28.9 us -> 2.64 us
    all_gather x1 -> x0, blocking collectives: 20 us -> none  [body(): row_vec = lax.all_gather(basis_block, 'col', axis=1, tiled=True)]
  transfers between devices with their start and end apart: 3 -> 0, of which waited for: 3 -> 0; matrix products, arithmetic and copies ran while one was open for 5% -> 0% of each run, Pallas kernels for 0% -> 0%
where the time goes in v1:
time: 66.4 us; the launch traced here: 66.1 us
  Pallas kernels  62.2 us (94%)
  local copies, waits for them, and re-layouts  2.64 us (4%)
  between operations  1.3 us (2%)
    pallas_call x1, Pallas kernels, step(): pl.pallas_call(body, out_shape=(jax.ShapeDtypeStruct((BLOCKS, K, TILE), F...  62.2 us
    unnamed x7, local copies, waits for them, and re-layouts  2.64 us

profile of v1, /device:TPU:1, one launch (start us, length us, event | category | flops | bytes accessed | tf_op | source)
XLA Modules:
  0.0 66.1 jit_solution(7764219810789171840)
XLA Ops:
  1.3 62.2 %lanczos.1 = (f32[16,4,128]{2,1,0:T(4,128)}, f32[4,4]{1,0:T(4,128)}, f32[4,4]{1,0:T(4,128)}) custom-call(s32[8]{0:T(128)} %rows.1, s32[8]{0:T(128)} %cols.1, s32[1]{0:T(128)S(6)} %copy.14.count, f32[4,4]{1,0:T(4,128)} %coupling.1, f32[8,128,128]{2,1,0:T(8,128)} %tiles_hbm.1, f32[16,128]{1,0:T(8,128)} %bitcast.13, f32[16,4,128]{2,1,0:T(4,128)} %bitcast.10, ...), custom_call_target="tpu_custom_call" | custom-call | tf_op jit(solution)/shard_map/lanczos/pallas_call | solution.py:359
  63.5 0.0 copy-start.1
  63.5 1.4 %copy.15 = f32[4,2048]{1,0:T(4,128)} copy(f32[4,2048]{1,0:T(4,128)} %bitcast.12) | data formatting | bytes 65536
  64.8 0.0 copy-done.1
  64.8 0.0 copy-start
  64.8 0.6 copy.16
  65.4 0.1 copy-done
  65.5 0.6 copy.17
Async XLA Ops:
  63.5 1.4 %copy-start.1 = (f32[4,4]{1,0:T(4,128)S(1)}, f32[4,4]{1,0:T(4,128)}, u32[]{:S(2)}) copy-start(f32[4,4]{1,0:T(4,128)} %get-tuple-element.13) | copy-start | bytes 196
  64.8 0.7 %copy-start = (f32[4,4]{1,0:T(4,128)S(1)}, f32[4,4]{1,0:T(4,128)}, u32[]{:S(2)}) copy-start(f32[4,4]{1,0:T(4,128)} %get-tuple-element.14) | copy-start | bytes 196

commit v2 on v1

--- a/solution.py
+++ b/solution.py
@@ -13,8 +13,17 @@
 BLOCKS = WIDTH // TILE
 CHUNK = BLOCKS + 1
 TOTAL = float(WIDTH * ROWS * COLS)
-REACH = {1: CHIPS // 2, -1: CHIPS // 2 - 1}
-HOP = 2
+TREE = {
+    0: (3, -3, 1, -1),
+    3: (6, 4, 2), -3: (-6, -4, -2),
+    6: (8, 7, 5), -6: (-7, -5),
+}
+FIRST, SECOND, THIRD = (1, -1, 3, -3), (2, -2, 4, -4, 6, -6), (5, -5, 7, -7, 8)
+RING = {0: 0, 1: 1, 2: 2, 3: 1}
+PLANE = sorted(
+    ((dx, dy) for dx in range(4) for dy in range(4) if dx or dy), key=lambda p: -RING[p[0]] - RING[p[1]]
+)
+COLUMN = sorted(range(1, CHIPS), key=lambda d: -min(d, CHIPS - d))
 
 
 def dot(a, b, trans_b=False):
@@ -77,22 +86,27 @@
 def body(rows, cols, count, coupling, tiles_hbm, energy_hbm, basis_hbm, prev_hbm,
          next_ref, alpha_ref, beta_ref,
          xcol, xrow, tiles, energy, prev, fsend, fbuf, dsend, dbuf, gather, red1, red2, msg,
-         local, xs, xr, hs, hr, ps, pr, fs, fr, gs, gr, ds, dr, as1, ar1, as2, ar2):
+         local, sent, xr, hr, pr, fr, gr, dr, ar1, ar2):
     i, j = lax.axis_index("row"), lax.axis_index("col")
     sib = (i + 1 - 2 * lax.rem(i, 2), j)
 
-    def chip(d):
-        return (lax.rem(i + 2 * d + ROWS, ROWS), j)
-
-    def plane(d):
-        return (i, lax.rem(j + d, COLS))
-
-    def send(src, dst, s, r, dev):
-        c = pltpu.make_async_remote_copy(
+    def chip(d, other=False):
+        core = lax.rem(i, 2)
+        return (2 * lax.rem(i // 2 + d + CHIPS, CHIPS) + (1 - core if other else core), j)
+
+    def plane(p):
+        return (i, 4 * lax.rem(j // 4 + p[0], 4) + lax.rem(lax.rem(j, 4) + p[1], 4))
+
+    def copy(src, dst, s, r, dev):
+        return pltpu.make_async_remote_copy(
             src_ref=src, dst_ref=dst, send_sem=s, recv_sem=r, device_id=dev, device_id_type=MESH
         )
-        c.start()
-        return c
+
+    def arrived(ref, sem):
+        copy(ref, ref, sem, sem, sib).wait_recv()
+
+    def left(ref, sem):
+        copy(ref, ref, sem, sem, sib).wait_send()
 
     loads = [
         pltpu.make_async_copy(basis_hbm, xcol.at[pl.ds(i * CHUNK, BLOCKS)], local.at[0]),
@@ -105,13 +119,9 @@
         c.start()
 
     barrier = pltpu.get_barrier_semaphore()
-    near = [chip(s * d) for d in range(1, HOP + 1) for s in (1, -1)] + [sib]
+    near = [chip(s * d) for d in (3, 2, 1) for s in (1, -1)] + [plane(p) for p in PLANE] + [sib]
     for dev in near:
         pl.semaphore_signal(barrier, inc=1, device_id=dev, device_id_type=MESH)
-
-    @pl.loop(1, COLS)
-    def _(d):
-        pl.semaphore_signal(barrier, inc=1, device_id=plane(d), device_id_type=MESH)
 
     sub = lax.broadcasted_iota(jnp.int32, (K, TILE), 0)
     lane = lax.broadcasted_iota(jnp.int32, (K, TILE), 1)
@@ -126,62 +136,36 @@
     xrow[j * CHUNK + BLOCKS] = places
     loads[0].wait()
     loads[1].wait()
-    pl.semaphore_wait(barrier, len(near) + COLS - 1)
-
-    def place(buf, slot):
-        return buf.at[pl.ds(slot * CHUNK, CHUNK)] if buf is xcol or buf is xrow else buf.at[slot]
-
-    def ring(buf, ssem, rsem, copies, base, s):
-        at = place(buf, lax.rem(i - 2 * s * base + 2 * ROWS, ROWS))
-        for d in range(HOP, 0, -1):
-            t = base + d
-            if t <= REACH[s]:
-                n = 2 * (t - 1) + (s < 0)
-                copies[(t, s)] = send(at, at, ssem.at[n], rsem.at[n], chip(s * d))
-
-    def share(buf, ssem, rsem, copies, t, s):
-        at = place(buf, lax.rem(i - 2 * s * t + 2 * ROWS, ROWS))
-        n = len(copies)
-        copies.append(send(at, at, ssem.at[n], rsem.at[n], sib))
-
-    def arrive(buf, sems, ssems, copies, shares, hops):
+    pl.semaphore_wait(barrier, len(near))
+
+    def place(buf, t):
+        slot = lax.rem(i - 2 * t + ROWS, ROWS)
+        return buf.at[pl.ds(slot * CHUNK, CHUNK)] if buf is xcol else buf.at[slot]
+
+    def onward(buf, n, rsem, hsem, t):
+        at = place(buf, t)
+        for u in TREE.get(t, ()):
+            copy(at, at, sent.at[n], rsem.at[u + CHIPS // 2 - 1], chip(u - t)).start()
+        copy(at, at, sent.at[n + 1], hsem.at[0], sib).start()
+
+    def arrive(buf, n, rsem, hsem, hops):
         for t in hops:
-            for s in (1, -1):
-                if t <= REACH[s]:
-                    copies[(t, s)].wait_recv()
-                    if t % HOP == 0:
-                        ring(buf, *sems, copies, t, s)
-        for t in hops:
-            for s in (1, -1):
-                if t <= REACH[s]:
-                    share(buf, *ssems, shares, t, s)
-
-    def over_plane(src, dst, ssem, rsem):
-        @pl.loop(1, COLS)
-        def _(d):
-            send(src, dst, ssem.at[d], rsem.at[d], plane(d))
-
-    def plane_wait(src, dst, ssem, rsem):
-        @pl.loop(1, COLS)
-        def _(d):
-            c = pltpu.make_async_remote_copy(
-                src_ref=src, dst_ref=dst, send_sem=ssem.at[d], recv_sem=rsem.at[d],
-                device_id=plane(d), device_id_type=MESH,
-            )
-            c.wait()
-
-    xc, xh, fc, fh = {}, [], {}, []
-    ring(xcol, xs, xr, xc, 0, 1)
-    ring(xcol, xs, xr, xc, 0, -1)
-    share(xcol, hs, hr, xh, 0, 1)
-    own = place(xrow, j)
-    over_plane(own, own, ps, pr)
+            arrived(place(buf, t), rsem.at[t + CHIPS // 2 - 1])
+            onward(buf, n, rsem, hsem, t)
+
+    def over_plane(src, dst, n, rsem):
+        for p in PLANE:
+            copy(src, dst, sent.at[n], rsem.at[0], plane(p)).start()
+
+    own = xrow.at[pl.ds(j * CHUNK, CHUNK)]
+    onward(xcol, 0, xr, hr, 0)
+    over_plane(own, own, 4, pr)
 
     for c in loads[2:]:
         c.wait()
 
-    arrive(xcol, (xs, xr), (hs, hr), xc, xh, (1, 2))
-    plane_wait(own, own, ps, pr)
+    arrive(xcol, 0, xr, hr, FIRST)
+    arrived(xrow.at[pl.ds(0, (COLS - 1) * CHUNK)], pr.at[0])
 
     for t in range(SLOTS):
         r = rows[t]
@@ -190,17 +174,12 @@
         for k in range(K):
             fsend[k, t : t + 1, :] = y[k : k + 1, :]
     fbuf[i] = fsend[...]
-    ring(fbuf, fs, fr, fc, 0, 1)
-    ring(fbuf, fs, fr, fc, 0, -1)
-    share(fbuf, gs, gr, fh, 0, 1)
-
-    arrive(xcol, (xs, xr), (hs, hr), xc, xh, (3, 4))
-    arrive(fbuf, (fs, fr), (gs, gr), fc, fh, (1, 2))
-    arrive(xcol, (xs, xr), (hs, hr), xc, xh, (5, 6))
-    arrive(fbuf, (fs, fr), (gs, gr), fc, fh, (3, 4))
-    arrive(xcol, (xs, xr), (hs, hr), xc, xh, (7, 8))
-    for c in xh:
-        c.wait()
+    onward(fbuf, 2, fr, gr, 0)
+
+    arrive(xcol, 0, xr, hr, SECOND)
+    arrive(fbuf, 2, fr, gr, FIRST)
+    arrive(xcol, 0, xr, hr, THIRD)
+    arrived(xcol.at[pl.ds(0, ROWS // 2 * CHUNK)], hr.at[0])
 
     for t in range(SLOTS):
         r = cols[t]
@@ -209,8 +188,8 @@
         for k in range(K):
             dsend[k, t : t + 1, :] = y[k : k + 1, :]
     dbuf[j] = dsend[...]
-    over_plane(dbuf.at[j], dbuf.at[j], ds, dr)
-    arrive(fbuf, (fs, fr), (gs, gr), fc, fh, (5, 6))
+    over_plane(dbuf.at[j], dbuf.at[j], 5, dr)
+    arrive(fbuf, 2, fr, gr, SECOND)
 
     at_cols = jnp.zeros((K, TILE), F32)
     for d in range(ROWS):
@@ -245,14 +224,13 @@
         for l in range(K):
             inner(4 * k + l, x[k], x[l])
 
-    arrive(fbuf, (fs, fr), (gs, gr), fc, fh, (7, 8))
-    for c in fh:
-        c.wait()
+    arrive(fbuf, 2, fr, gr, THIRD)
+    arrived(fbuf.at[pl.ds(0, ROWS // 2)], gr.at[0])
     for k in range(K):
         low = fbuf[0:16, k].reshape(TILE, TILE)
         high = fbuf[16:32, k].reshape(TILE, TILE)
         res[k] = res[k] + (dot(hot_low, low) + dot(hot_high, high))
-    plane_wait(dbuf.at[j], dbuf.at[j], ds, dr)
+    arrived(dbuf.at[pl.ds(0, COLS - 1)], dr.at[0])
     for k in range(K):
         res[k] = res[k] + dot(hot_row, dbuf[:, k].reshape(TILE, TILE))
 
@@ -265,25 +243,17 @@
     msg[0] = here[0:1]
     red1[j] = here[0:1]
 
-    over_plane(msg.at[0], red1.at[j], as1, ar1)
-    plane_wait(msg.at[0], red1.at[j], as1, ar1)
+    over_plane(msg.at[0], red1.at[j], 6, ar1)
+    arrived(red1.at[pl.ds(0, COLS - 1)], ar1.at[0])
     part = sum_pairs(red1[...].reshape(COLS, TILE))
     msg[1] = part[0:1]
     red2[i] = part[0:1]
 
-    def column(d):
-        return pltpu.make_async_remote_copy(
-            src_ref=msg.at[1], dst_ref=red2.at[i], send_sem=as2.at[d], recv_sem=ar2.at[d],
-            device_id=(lax.rem(i + d, ROWS), j), device_id_type=MESH,
-        )
-
-    @pl.loop(1, ROWS)
-    def _(d):
-        column(d).start()
-
-    @pl.loop(1, ROWS)
-    def _(d):
-        column(d).wait()
+    for d in COLUMN:
+        for other in (False, True):
+            copy(msg.at[1], red2.at[i], sent.at[7], ar2.at[0], chip(d, other)).start()
+    copy(msg.at[1], red2.at[i], sent.at[7], ar2.at[0], sib).start()
+    arrived(red2.at[pl.ds(0, ROWS - 1)], ar2.at[0])
 
     sums = sum_pairs(red2[...].reshape(ROWS, TILE)) * (1.0 / TOTAL)
 
@@ -346,8 +316,24 @@
     alpha_ref[...] = a
     beta_ref[...] = b
 
-    for c in list(xc.values()) + list(fc.values()):
-        c.wait_send()
+    left(xcol.at[pl.ds(0, (CHIPS - 1) * CHUNK)], sent.at[0])
+    left(xcol.at[pl.ds(0, CHIPS * CHUNK)], sent.at[1])
+    left(fbuf.at[pl.ds(0, CHIPS - 1)], sent.at[2])
+    left(fbuf.at[pl.ds(0, CHIPS)], sent.at[3])
+    left(xrow.at[pl.ds(0, (COLS - 1) * CHUNK)], sent.at[4])
+    left(dbuf.at[pl.ds(0, COLS - 1)], sent.at[5])
+    left(red1.at[pl.ds(0, COLS - 1)], sent.at[6])
+    left(red2.at[pl.ds(0, ROWS - 1)], sent.at[7])
+
+
+def hand_over(*refs):
+    n = len(refs) // 2
+    sems = refs[-1]
+    copies = [pltpu.make_async_copy(refs[k], refs[n + k], sems.at[k]) for k in range(n)]
+    for c in copies:
+        c.start()
+    for c in copies:
+        c.wait()
 
 
 def step(tiles, tile_rows, tile_cols, tile_count, energy, basis_block, previous_block, coupling):
@@ -380,12 +366,10 @@
             pltpu.VMEM((ROWS, 1, TILE), F32),
             pltpu.VMEM((2, 1, TILE), F32),
             dma((5,)),
-            dma((CHIPS,)), dma((CHIPS,)), dma((CHIPS,)), dma((CHIPS,)),
-            dma((COLS,)), dma((COLS,)),
-            dma((CHIPS,)), dma((CHIPS,)), dma((CHIPS,)), dma((CHIPS,)),
-            dma((COLS,)), dma((COLS,)),
-            dma((COLS,)), dma((COLS,)),
-            dma((ROWS,)), dma((ROWS,)),
+            dma((8,)),
+            dma((CHIPS,)), dma((1,)), dma((1,)),
+            dma((CHIPS,)), dma((1,)), dma((1,)),
+            dma((1,)), dma((1,)),
         ],
         compiler_params=pltpu.CompilerParams(
             collective_id=0, has_side_effects=True, vmem_limit_bytes=56 << 20
@@ -395,6 +379,16 @@
         tile_rows, tile_cols, tile_count, coupling, tiles, energy.reshape(BLOCKS, TILE),
         blocked(basis_block), blocked(previous_block),
     )
+    results = (out, alpha, beta)
+    out, alpha, beta = pl.pallas_call(
+        hand_over,
+        out_shape=tuple(jax.ShapeDtypeStruct(r.shape, F32) for r in results),
+        in_specs=[hbm] * 3,
+        out_specs=(hbm,) * 3,
+        scratch_shapes=[dma((3,))],
+        compiler_params=pltpu.CompilerParams(vmem_limit_bytes=56 << 20),
+        name="hand_over",
+    )(*results)
     return out.transpose(1, 0, 2).reshape(K, WIDTH), alpha, beta
 
 

time: 66.4 us -> 57.3 us (0.86)
  Pallas kernels: 62.2 us -> 55.8 us
  local copies, waits for them, and re-layouts: 2.64 us -> 0 us
    pallas_call x1, Pallas kernels: 62.2 us -> 53.6 us  [step(): pl.pallas_call(body, out_shape=(jax.ShapeDtypeStruct((BLOCKS, K, TILE), F...]
    unnamed x7 -> x0, local copies, waits for them, and re-layouts: 2.64 us -> none
    pallas_call x0 -> x1, Pallas kernels: none -> 2.25 us  [step(): pl.pallas_call(hand_over, out_shape=tuple((jax.ShapeDtypeStruct(r.shape,...]
where the time goes in v2:
time: 57.3 us; the launch traced here: 57.1 us
  Pallas kernels  55.8 us (97%)
  between operations  1.29 us (2%)
    pallas_call x1, Pallas kernels, step(): pl.pallas_call(body, out_shape=(jax.ShapeDtypeStruct((BLOCKS, K, TILE), F...  53.6 us
    pallas_call x1, Pallas kernels, step(): pl.pallas_call(hand_over, out_shape=tuple((jax.ShapeDtypeStruct(r.shape,...  2.25 us

profile of v2, /device:TPU:1, one launch (start us, length us, event | category | flops | bytes accessed | tf_op | source)
XLA Modules:
  0.0 57.1 jit_solution(6492092110302102245)
XLA Ops:
  1.3 53.6 %lanczos.1 = (f32[16,4,128]{2,1,0:T(4,128)}, f32[4,4]{1,0:T(4,128)}, f32[4,4]{1,0:T(4,128)}) custom-call(s32[8]{0:T(128)} %rows.1, s32[8]{0:T(128)} %cols.1, s32[1]{0:T(128)S(6)} %copy.11.count, f32[4,4]{1,0:T(4,128)} %coupling.1, f32[8,128,128]{2,1,0:T(8,128)} %tiles_hbm.1, f32[16,128]{1,0:T(8,128)} %bitcast.12, f32[16,4,128]{2,1,0:T(4,128)} %bitcast.10, ...), custom_call_target="tpu_custom_call" | custom-call | tf_op jit(solution)/shard_map/lanczos/pallas_call | solution.py:345
  54.8 2.2 %hand_over.1 = (f32[16,4,128]{2,1,0:T(4,128)}, f32[4,4]{1,0:T(4,128)}, f32[4,4]{1,0:T(4,128)}) custom-call(f32[16,4,128]{2,1,0:T(4,128)} %get-tuple-element.9.refs_0_, f32[4,4]{1,0:T(4,128)} %get-tuple-element.10.refs_1_, f32[4,4]{1,0:T(4,128)} %get-tuple-element.11.refs_2_), custom_call_target="tpu_custom_call" | custom-call | tf_op jit(solution)/shard_map/hand_over/pallas_call | solution.py:383

commit v3 on v2

--- a/solution.py
+++ b/solution.py
@@ -31,6 +31,28 @@
     return lax.dot_general(a, b, dims, precision=HIGH, preferred_element_type=F32)
 
 
+def thirds(a):
+    parts = []
+    for _ in range(3):
+        p = a.astype(jnp.bfloat16).astype(F32)
+        parts.append(p)
+        a = a - p
+    return parts
+
+
+def split_tile(tile, out):
+    for n, p in enumerate(thirds(tile)):
+        out[n * TILE : (n + 1) * TILE, :] = p.astype(jnp.bfloat16)
+
+
+def product(x, tile):
+    left = jnp.concatenate(thirds(x) + [jnp.zeros_like(x)], axis=0).astype(jnp.bfloat16)
+    y = lax.dot_general(
+        jnp.concatenate([left] * 3, axis=1), tile, (((1,), (0,)), ((), ())), preferred_element_type=F32
+    )
+    return (y[8:12] + y[4:8]) + y[0:4]
+
+
 def two_sum(a, b):
     s = a + b
     t = s - a
@@ -67,13 +89,11 @@
     return x + jnp.where(lane >= 64, pltpu.roll(e, 64, 1), 0.0)
 
 
-def pick(row, base, stride_m, stride_k, stride_l, shift=0):
-    src = lax.broadcasted_iota(jnp.int32, (TILE, TILE), 0)
-    lane = lax.broadcasted_iota(jnp.int32, (TILE, TILE), 1)
-    m, k, l = lane // 16, (lane // 4) % 4, lane % 4
-    want = base + shift + stride_m * m + stride_k * k + stride_l * l
-    hot = jnp.where((src == want) & (lane < 64), 1.0, 0.0).astype(F32)
-    return dot(row, hot)
+def pick(row, base, stride_m, stride_k, stride_l):
+    lane = lax.broadcasted_iota(jnp.int32, (8, TILE), 1)
+    m, k, l = lane // 16 % 4, lane // 4 % 4, lane % 4
+    src = base + stride_m * m + stride_k * k + stride_l * l
+    return jnp.take_along_axis(row, src, axis=1, mode="promise_in_bounds")
 
 
 def fold_m(x, e):
@@ -83,9 +103,9 @@
     return x, e
 
 
-def body(rows, cols, count, coupling, tiles_hbm, energy_hbm, basis_hbm, prev_hbm,
+def body(count, rows_hbm, cols_hbm, coupling_hbm, tiles_hbm, energy_hbm, basis_hbm, prev_hbm,
          next_ref, alpha_ref, beta_ref,
-         xcol, xrow, tiles, energy, prev, fsend, fbuf, dsend, dbuf, gather, red1, red2, msg,
+         rows, cols, coupling, xcol, xrow, tiles, parts, flipped, energy, prev, fsend, fbuf, dsend, dbuf, gather, red1, red2, msg,
          local, sent, xr, hr, pr, fr, gr, dr, ar1, ar2):
     i, j = lax.axis_index("row"), lax.axis_index("col")
     sib = (i + 1 - 2 * lax.rem(i, 2), j)
@@ -114,6 +134,9 @@
         pltpu.make_async_copy(tiles_hbm, tiles, local.at[2]),
         pltpu.make_async_copy(energy_hbm, energy, local.at[3]),
         pltpu.make_async_copy(prev_hbm, prev, local.at[4]),
+        pltpu.make_async_copy(rows_hbm, rows, local.at[5]),
+        pltpu.make_async_copy(cols_hbm, cols, local.at[6]),
+        pltpu.make_async_copy(coupling_hbm, coupling, local.at[7]),
     ]
     for c in loads:
         c.start()
@@ -122,6 +145,9 @@
     near = [chip(s * d) for d in (3, 2, 1) for s in (1, -1)] + [plane(p) for p in PLANE] + [sib]
     for dev in near:
         pl.semaphore_signal(barrier, inc=1, device_id=dev, device_id_type=MESH)
+
+    for c in loads[5:]:
+        c.wait()
 
     sub = lax.broadcasted_iota(jnp.int32, (K, TILE), 0)
     lane = lax.broadcasted_iota(jnp.int32, (K, TILE), 1)
@@ -161,8 +187,10 @@
     onward(xcol, 0, xr, hr, 0)
     over_plane(own, own, 4, pr)
 
-    for c in loads[2:]:
+    for c in loads[2:5]:
         c.wait()
+    for t in range(SLOTS):
+        split_tile(tiles[t], parts.at[t])
 
     arrive(xcol, 0, xr, hr, FIRST)
     arrived(xrow.at[pl.ds(0, (COLS - 1) * CHUNK)], pr.at[0])
@@ -170,26 +198,28 @@
     for t in range(SLOTS):
         r = rows[t]
         v = xrow[r + lax.shift_right_logical(r, 4)]
-        y = dot(v, tiles[t])
+        y = product(v, parts[t])
         for k in range(K):
             fsend[k, t : t + 1, :] = y[k : k + 1, :]
     fbuf[i] = fsend[...]
     onward(fbuf, 2, fr, gr, 0)
+    for t in range(SLOTS):
+        split_tile(tiles[t].T, flipped.at[t])
 
     arrive(xcol, 0, xr, hr, SECOND)
     arrive(fbuf, 2, fr, gr, FIRST)
     arrive(xcol, 0, xr, hr, THIRD)
+    arrive(fbuf, 2, fr, gr, SECOND)
     arrived(xcol.at[pl.ds(0, ROWS // 2 * CHUNK)], hr.at[0])
 
     for t in range(SLOTS):
         r = cols[t]
         v = xcol[r + lax.shift_right_logical(r, 4)]
-        y = dot(v, tiles[t], trans_b=True)
+        y = product(v, flipped[t])
         for k in range(K):
             dsend[k, t : t + 1, :] = y[k : k + 1, :]
     dbuf[j] = dsend[...]
     over_plane(dbuf.at[j], dbuf.at[j], 5, dr)
-    arrive(fbuf, 2, fr, gr, SECOND)
 
     at_cols = jnp.zeros((K, TILE), F32)
     for d in range(ROWS):
@@ -257,9 +287,9 @@
 
     sums = sum_pairs(red2[...].reshape(ROWS, TILE)) * (1.0 / TOTAL)
 
-    g_km, g_km_low = pick(sums, 0, 1, 4, 0), pick(sums, 0, 1, 4, 0, 64)
+    g_km, g_km_low = pick(sums, 0, 1, 4, 0), pick(sums, 64, 1, 4, 0)
     f_ml = pick(sums, 16, 4, 0, 1)
-    f_mk, f_mk_low = pick(sums, 16, 4, 1, 0), pick(sums, 16, 4, 1, 0, 64)
+    f_mk, f_mk_low = pick(sums, 16, 4, 1, 0), pick(sums, 80, 4, 1, 0)
     first = pltpu.roll(sums, TILE - 16, 1)
     gf, _ = fold_m(g_km * f_ml, jnp.zeros_like(g_km))
     alpha = first + (first - gf)
@@ -337,24 +367,33 @@
 
 
 def step(tiles, tile_rows, tile_cols, tile_count, energy, basis_block, previous_block, coupling):
-    vmem, smem, hbm = (pl.BlockSpec(memory_space=m) for m in (pltpu.VMEM, pltpu.SMEM, pl.ANY))
+    vmem, hbm = (pl.BlockSpec(memory_space=m) for m in (pltpu.VMEM, pl.ANY))
     dma = pltpu.SemaphoreType.DMA
     def blocked(a):
         return a.reshape(K, BLOCKS, TILE).transpose(1, 0, 2)
 
+    operands = (
+        tile_rows, tile_cols, coupling, tiles, energy.reshape(BLOCKS, TILE),
+        blocked(basis_block), blocked(previous_block),
+    )
     out, alpha, beta = pl.pallas_call(
         body,
         out_shape=(
-            jax.ShapeDtypeStruct((BLOCKS, K, TILE), F32),
-            jax.ShapeDtypeStruct((K, K), F32),
-            jax.ShapeDtypeStruct((K, K), F32),
+            pltpu.VMEM((BLOCKS, K, TILE), F32),
+            pltpu.VMEM((K, K), F32),
+            pltpu.VMEM((K, K), F32),
         ),
-        in_specs=[smem] * 4 + [hbm] * 4,
+        in_specs=[pl.BlockSpec(memory_space=pltpu.SMEM)] + [hbm] * 7,
         out_specs=(vmem, vmem, vmem),
         scratch_shapes=[
+            pltpu.SMEM((SLOTS,), jnp.int32),
+            pltpu.SMEM((SLOTS,), jnp.int32),
+            pltpu.SMEM((K, K), F32),
             pltpu.VMEM((ROWS * CHUNK, K, TILE), F32),
             pltpu.VMEM((COLS * CHUNK, K, TILE), F32),
             pltpu.VMEM((SLOTS, TILE, TILE), F32),
+            pltpu.VMEM((SLOTS, 3 * TILE, TILE), jnp.bfloat16),
+            pltpu.VMEM((SLOTS, 3 * TILE, TILE), jnp.bfloat16),
             pltpu.VMEM((BLOCKS, TILE), F32),
             pltpu.VMEM((BLOCKS, K, TILE), F32),
             pltpu.VMEM((K, SLOTS, TILE), F32),
@@ -365,20 +404,17 @@
             pltpu.VMEM((COLS, 1, TILE), F32),
             pltpu.VMEM((ROWS, 1, TILE), F32),
             pltpu.VMEM((2, 1, TILE), F32),
-            dma((5,)),
+            dma((8,)),
             dma((8,)),
             dma((CHIPS,)), dma((1,)), dma((1,)),
             dma((CHIPS,)), dma((1,)), dma((1,)),
             dma((1,)), dma((1,)),
         ],
         compiler_params=pltpu.CompilerParams(
-            collective_id=0, has_side_effects=True, vmem_limit_bytes=56 << 20
+            collective_id=0, has_side_effects=True, vmem_limit_bytes=32 << 20
         ),
         name="lanczos",
-    )(
-        tile_rows, tile_cols, tile_count, coupling, tiles, energy.reshape(BLOCKS, TILE),
-        blocked(basis_block), blocked(previous_block),
-    )
+    )(tile_count, *(pltpu.with_memory_space_constraint(a, pltpu.HBM) for a in operands))
     results = (out, alpha, beta)
     out, alpha, beta = pl.pallas_call(
         hand_over,
@@ -386,7 +422,7 @@
         in_specs=[hbm] * 3,
         out_specs=(hbm,) * 3,
         scratch_shapes=[dma((3,))],
-        compiler_params=pltpu.CompilerParams(vmem_limit_bytes=56 << 20),
+        compiler_params=pltpu.CompilerParams(vmem_limit_bytes=1 << 20),
         name="hand_over",
     )(*results)
     return out.transpose(1, 0, 2).reshape(K, WIDTH), alpha, beta

time: 57.3 us -> 54.5 us (0.951)
  Pallas kernels: 55.8 us -> 53.1 us
    pallas_call x1, Pallas kernels: 2.25 us -> 0.65 us  [step(): pl.pallas_call(hand_over, out_shape=tuple((jax.ShapeDtypeStruct(r.shape,...]
    pallas_call x1, Pallas kernels: 53.6 us -> 52.4 us  [step(): pl.pallas_call(body, out_shape=(pltpu.VMEM((BLOCKS, K, TILE), F32), pltpu...]
where the time goes in v3:
time: 54.5 us; the launch traced here: 54.3 us
  Pallas kernels  53.1 us (97%)
  between operations  1.29 us (2%)
    pallas_call x1, Pallas kernels, step(): pl.pallas_call(body, out_shape=(pltpu.VMEM((BLOCKS, K, TILE), F32), pltpu...  52.4 us

profile of v3, /device:TPU:1, one launch (start us, length us, event | category | flops | bytes accessed | tf_op | source)
XLA Modules:
  0.0 54.3 jit_solution(13998615334095637498)
XLA Ops:
  1.3 52.4 %lanczos.1 = (f32[16,4,128]{2,1,0:T(4,128)S(1)}, f32[4,4]{1,0:T(4,128)S(1)}, f32[4,4]{1,0:T(4,128)S(1)}) custom-call(s32[1]{0:T(128)S(6)} %copy.11.count, s32[8]{0:T(128)} %rows_hbm.1, s32[8]{0:T(128)} %cols_hbm.1, f32[4,4]{1,0:T(4,128)} %coupling_hbm.1, f32[8,128,128]{2,1,0:T(8,128)} %tiles_hbm.1, f32[16,128]{1,0:T(8,128)} %bitcast.12, ...), custom_call_target="tpu_custom_call" | custom-call | tf_op jit(solution)/shard_map/lanczos/pallas_call | solution.py:379
  53.7 0.6 %hand_over.1 = (f32[16,4,128]{2,1,0:T(4,128)}, f32[4,4]{1,0:T(4,128)}, f32[4,4]{1,0:T(4,128)}) custom-call(f32[16,4,128]{2,1,0:T(4,128)S(1)} %get-tuple-element.9.refs_0_, f32[4,4]{1,0:T(4,128)S(1)} %get-tuple-element.10.refs_1_, f32[4,4]{1,0:T(4,128)S(1)} %get-tuple-element.11.refs_2_), custom_call_target="tpu_custom_call" | custom-call | tf_op jit(solution)/shard_map/hand_over/pallas_call | solution.py:419

commit v4 on v3

--- a/solution.py
+++ b/solution.py
@@ -18,7 +18,9 @@
     3: (6, 4, 2), -3: (-6, -4, -2),
     6: (8, 7, 5), -6: (-7, -5),
 }
-FIRST, SECOND, THIRD = (1, -1, 3, -3), (2, -2, 4, -4, 6, -6), (5, -5, 7, -7, 8)
+WAVES = (1, -1, 3, -3), (2, -2, 4, -4, 6, -6), (5, -5, 7, -7, 8)
+LIST_TREE = {0: (3, -3, 1, -1), 3: (6, 4, 2), -3: (-6, -4, -2), 6: (8, 7, 5), -6: (-7, -5)}
+LIST_WAVES = ((1, -1, 3, -3), (2, -2, 4, -4, 6, -6), (5, -5, 7, -7, 8))
 RING = {0: 0, 1: 1, 2: 2, 3: 1}
 PLANE = sorted(
     ((dx, dy) for dx in range(4) for dy in range(4) if dx or dy), key=lambda p: -RING[p[0]] - RING[p[1]]
@@ -170,7 +172,7 @@
 
     def onward(buf, n, rsem, hsem, t):
         at = place(buf, t)
-        for u in TREE.get(t, ()):
+        for u in (TREE if buf is xcol else LIST_TREE).get(t, ()):
             copy(at, at, sent.at[n], rsem.at[u + CHIPS // 2 - 1], chip(u - t)).start()
         copy(at, at, sent.at[n + 1], hsem.at[0], sib).start()
 
@@ -192,7 +194,9 @@
     for t in range(SLOTS):
         split_tile(tiles[t], parts.at[t])
 
-    arrive(xcol, 0, xr, hr, FIRST)
+    for t in range(SLOTS):
+        split_tile(tiles[t].T, flipped.at[t])
+    arrive(xcol, 0, xr, hr, WAVES[0])
     arrived(xrow.at[pl.ds(0, (COLS - 1) * CHUNK)], pr.at[0])
 
     for t in range(SLOTS):
@@ -203,13 +207,10 @@
             fsend[k, t : t + 1, :] = y[k : k + 1, :]
     fbuf[i] = fsend[...]
     onward(fbuf, 2, fr, gr, 0)
-    for t in range(SLOTS):
-        split_tile(tiles[t].T, flipped.at[t])
-
-    arrive(xcol, 0, xr, hr, SECOND)
-    arrive(fbuf, 2, fr, gr, FIRST)
-    arrive(xcol, 0, xr, hr, THIRD)
-    arrive(fbuf, 2, fr, gr, SECOND)
+
+    arrive(xcol, 0, xr, hr, WAVES[1])
+    arrive(fbuf, 2, fr, gr, LIST_WAVES[0])
+    arrive(xcol, 0, xr, hr, WAVES[2])
     arrived(xcol.at[pl.ds(0, ROWS // 2 * CHUNK)], hr.at[0])
 
     for t in range(SLOTS):
@@ -220,6 +221,7 @@
             dsend[k, t : t + 1, :] = y[k : k + 1, :]
     dbuf[j] = dsend[...]
     over_plane(dbuf.at[j], dbuf.at[j], 5, dr)
+    arrive(fbuf, 2, fr, gr, LIST_WAVES[1])
 
     at_cols = jnp.zeros((K, TILE), F32)
     for d in range(ROWS):
@@ -254,7 +256,7 @@
         for l in range(K):
             inner(4 * k + l, x[k], x[l])
 
-    arrive(fbuf, 2, fr, gr, THIRD)
+    arrive(fbuf, 2, fr, gr, LIST_WAVES[2])
     arrived(fbuf.at[pl.ds(0, ROWS // 2)], gr.at[0])
     for k in range(K):
         low = fbuf[0:16, k].reshape(TILE, TILE)

time: 54.5 us -> 53.1 us (0.974)
  Pallas kernels: 53.1 us -> 51.7 us
    pallas_call x1, Pallas kernels: 52.4 us -> 51 us  [step(): pl.pallas_call(body, out_shape=(pltpu.VMEM((BLOCKS, K, TILE), F32), pltpu...]
where the time goes in v4:
time: 53.1 us; the launch traced here: 53 us
  Pallas kernels  51.7 us (97%)
  between operations  1.29 us (2%)
    pallas_call x1, Pallas kernels, step(): pl.pallas_call(body, out_shape=(pltpu.VMEM((BLOCKS, K, TILE), F32), pltpu...  51 us

profile of v4, /device:TPU:1, one launch (start us, length us, event | category | flops | bytes accessed | tf_op | source)
XLA Modules:
  0.0 53.0 jit_solution(4894041802976003159)
XLA Ops:
  1.3 51.0 %lanczos.1 = (f32[16,4,128]{2,1,0:T(4,128)S(1)}, f32[4,4]{1,0:T(4,128)S(1)}, f32[4,4]{1,0:T(4,128)S(1)}) custom-call(s32[1]{0:T(128)S(6)} %copy.11.count, s32[8]{0:T(128)} %rows_hbm.1, s32[8]{0:T(128)} %cols_hbm.1, f32[4,4]{1,0:T(4,128)} %coupling_hbm.1, f32[8,128,128]{2,1,0:T(8,128)} %tiles_hbm.1, f32[16,128]{1,0:T(8,128)} %bitcast.12, ...), custom_call_target="tpu_custom_call" | custom-call | tf_op jit(solution)/shard_map/lanczos/pallas_call | solution.py:381
  52.3 0.6 %hand_over.1 = (f32[16,4,128]{2,1,0:T(4,128)}, f32[4,4]{1,0:T(4,128)}, f32[4,4]{1,0:T(4,128)}) custom-call(f32[16,4,128]{2,1,0:T(4,128)S(1)} %get-tuple-element.9.refs_0_, f32[4,4]{1,0:T(4,128)S(1)} %get-tuple-element.10.refs_1_, f32[4,4]{1,0:T(4,128)S(1)} %get-tuple-element.11.refs_2_), custom_call_target="tpu_custom_call" | custom-call | tf_op jit(solution)/shard_map/hand_over/pallas_call | solution.py:421

commit v5 on v4

--- a/solution.py
+++ b/solution.py
@@ -93,16 +93,17 @@
 
 def pick(row, base, stride_m, stride_k, stride_l):
     lane = lax.broadcasted_iota(jnp.int32, (8, TILE), 1)
-    m, k, l = lane // 16 % 4, lane // 4 % 4, lane % 4
-    src = base + stride_m * m + stride_k * k + stride_l * l
+    src = base + stride_k * (lane // 4 % 4) + stride_l * (lane % 4)
+    return [jnp.take_along_axis(row, src + stride_m * m, axis=1, mode="promise_in_bounds") for m in range(K)]
+
+
+def entry(row, k, l):
+    src = jnp.full((8, TILE), 4 * k + l, jnp.int32)
     return jnp.take_along_axis(row, src, axis=1, mode="promise_in_bounds")
 
 
-def fold_m(x, e):
-    for s in (32, 16):
-        x, r = two_sum(x, pltpu.roll(x, TILE - s, 1))
-        e = e + pltpu.roll(e, TILE - s, 1) + r
-    return x, e
+def times(v, plane):
+    return (plane.reshape(2, 8, TILE) * v).reshape(BLOCKS, TILE)
 
 
 def body(count, rows_hbm, cols_hbm, coupling_hbm, tiles_hbm, energy_hbm, basis_hbm, prev_hbm,
@@ -292,25 +293,28 @@
     g_km, g_km_low = pick(sums, 0, 1, 4, 0), pick(sums, 64, 1, 4, 0)
     f_ml = pick(sums, 16, 4, 0, 1)
     f_mk, f_mk_low = pick(sums, 16, 4, 1, 0), pick(sums, 80, 4, 1, 0)
-    first = pltpu.roll(sums, TILE - 16, 1)
-    gf, _ = fold_m(g_km * f_ml, jnp.zeros_like(g_km))
+    first, first_low = pltpu.roll(sums, TILE - 16, 1), pltpu.roll(sums, TILE - 80, 1)
+    resid, resid_low = pltpu.roll(sums, TILE - 32, 1), pltpu.roll(sums, TILE - 96, 1)
+    gf = (g_km[0] * f_ml[0] + g_km[1] * f_ml[1]) + (g_km[2] * f_ml[2] + g_km[3] * f_ml[3])
     alpha = first + (first - gf)
     a_ml, a_mk = pick(alpha, 0, 4, 0, 1), pick(alpha, 0, 4, 1, 0)
-    p, e = two_prod(g_km, a_ml)
-    p, e = fold_m(p, e + g_km_low * a_ml)
-    p, r = two_sum(p, -first)
-    e = e + r - pltpu.roll(sums, TILE - 80, 1)
+    p, e = -first, -first_low
+    for m in range(K):
+        q, r = two_prod(g_km[m], a_ml[m])
+        p, t = two_sum(p, q)
+        e = e + (r + t + g_km_low[m] * a_ml[m])
     p, e = two_sum(p, e)
     t_ml, t_ml_low = pick(p, 0, 4, 0, 1), pick(e, 0, 4, 0, 1)
-    p, e = two_prod(a_mk, t_ml)
-    q, r = two_prod(-f_mk, a_ml)
-    p, s = two_sum(p, q)
-    p, e = fold_m(p, e + r + s + a_mk * t_ml_low - f_mk_low * a_ml)
-    p, r = two_sum(p, pltpu.roll(sums, TILE - 32, 1))
-    gram = p + (e + r + pltpu.roll(sums, TILE - 96, 1))
-
-    def entry(v, k, l):
-        return v[0:1, 4 * k + l : 4 * k + l + 1]
+    p, e = resid, resid_low
+    for m in range(K):
+        q, r = two_prod(-f_mk[m], a_ml[m])
+        p, t = two_sum(p, q)
+        e = e + (r + t - f_mk_low[m] * a_ml[m])
+    for m in range(K):
+        q, r = two_prod(a_mk[m], t_ml[m])
+        p, t = two_sum(p, q)
+        e = e + (r + t + a_mk[m] * t_ml_low[m])
+    gram = p + e
 
     low = {}
     inv = []
@@ -318,8 +322,8 @@
         d = entry(gram, k, k)
         for m in range(k):
             d = d - low[k, m] * low[k, m]
-        low[k, k] = jnp.sqrt(d)
-        inv.append(1.0 / low[k, k])
+        inv.append(lax.rsqrt(d))
+        low[k, k] = d * inv[k]
         for n in range(k + 1, K):
             v = entry(gram, n, k)
             for m in range(k):
@@ -330,23 +334,23 @@
     for l in range(K):
         r = res[l]
         for k in range(K):
-            r = r - entry(alpha, k, l) * x[k]
+            r = r - times(entry(alpha, k, l), x[k])
         for m in range(l):
-            r = r - low[l, m] * done[m]
-        done.append(r * inv[l])
+            r = r - times(low[l, m], done[m])
+        done.append(times(inv[l], r))
     for k in range(K):
         next_ref[:, k, :] = done[k]
 
-    row4 = lax.broadcasted_iota(jnp.int32, (K, K), 0)
-    col4 = lax.broadcasted_iota(jnp.int32, (K, K), 1)
-    a, b = jnp.zeros((K, K), F32), jnp.zeros((K, K), F32)
+    sub = lax.broadcasted_iota(jnp.int32, (8, TILE), 0)
+    lane = lax.broadcasted_iota(jnp.int32, (8, TILE), 1)
+    a, b = jnp.zeros((8, TILE), F32), jnp.zeros((8, TILE), F32)
     for k in range(K):
         for l in range(K):
-            a = jnp.where((row4 == k) & (col4 == l), entry(alpha, k, l), a)
+            a = jnp.where((sub == k) & (lane == l), entry(alpha, k, l), a)
             if l >= k:
-                b = jnp.where((row4 == k) & (col4 == l), low[l, k], b)
-    alpha_ref[...] = a
-    beta_ref[...] = b
+                b = jnp.where((sub == k) & (lane == l), low[l, k], b)
+    alpha_ref[...] = a[0:K, 0:K]
+    beta_ref[...] = b[0:K, 0:K]
 
     left(xcol.at[pl.ds(0, (CHIPS - 1) * CHUNK)], sent.at[0])
     left(xcol.at[pl.ds(0, CHIPS * CHUNK)], sent.at[1])

time: 53.1 us -> 52.2 us (0.983)
  Pallas kernels: 51.7 us -> 50.8 us
    pallas_call x1, Pallas kernels: 51 us -> 50.2 us  [step(): pl.pallas_call(body, out_shape=(pltpu.VMEM((BLOCKS, K, TILE), F32), pltpu...]
where the time goes in v5:
time: 52.2 us; the launch traced here: 52.1 us
  Pallas kernels  50.8 us (97%)
  between operations  1.29 us (2%)
    pallas_call x1, Pallas kernels, step(): pl.pallas_call(body, out_shape=(pltpu.VMEM((BLOCKS, K, TILE), F32), pltpu...  50.2 us

profile of v5, /device:TPU:1, one launch (start us, length us, event | category | flops | bytes accessed | tf_op | source)
XLA Modules:
  0.0 52.1 jit_solution(3378022328513110854)
XLA Ops:
  1.3 50.2 %lanczos.1 = (f32[16,4,128]{2,1,0:T(4,128)S(1)}, f32[4,4]{1,0:T(4,128)S(1)}, f32[4,4]{1,0:T(4,128)S(1)}) custom-call(s32[1]{0:T(128)S(6)} %copy.11.count, s32[8]{0:T(128)} %rows_hbm.1, s32[8]{0:T(128)} %cols_hbm.1, f32[4,4]{1,0:T(4,128)} %coupling_hbm.1, f32[8,128,128]{2,1,0:T(8,128)} %tiles_hbm.1, f32[16,128]{1,0:T(8,128)} %bitcast.12, ...), custom_call_target="tpu_custom_call" | custom-call | tf_op jit(solution)/shard_map/lanczos/pallas_call | solution.py:385
  51.5 0.6 %hand_over.1 = (f32[16,4,128]{2,1,0:T(4,128)}, f32[4,4]{1,0:T(4,128)}, f32[4,4]{1,0:T(4,128)}) custom-call(f32[16,4,128]{2,1,0:T(4,128)S(1)} %get-tuple-element.9.refs_0_, f32[4,4]{1,0:T(4,128)S(1)} %get-tuple-element.10.refs_1_, f32[4,4]{1,0:T(4,128)S(1)} %get-tuple-element.11.refs_2_), custom_call_target="tpu_custom_call" | custom-call | tf_op jit(solution)/shard_map/hand_over/pallas_call | solution.py:425

commit v6 on v5

--- a/solution.py
+++ b/solution.py
@@ -18,9 +18,9 @@
     3: (6, 4, 2), -3: (-6, -4, -2),
     6: (8, 7, 5), -6: (-7, -5),
 }
-WAVES = (1, -1, 3, -3), (2, -2, 4, -4, 6, -6), (5, -5, 7, -7, 8)
+WAVES = (3, -3, 1, -1), (6, -6, 2, -2, 4, -4), (5, -5, 7, -7, 8)
 LIST_TREE = {0: (3, -3, 1, -1), 3: (6, 4, 2), -3: (-6, -4, -2), 6: (8, 7, 5), -6: (-7, -5)}
-LIST_WAVES = ((1, -1, 3, -3), (2, -2, 4, -4, 6, -6), (5, -5, 7, -7, 8))
+LIST_WAVES = ((3, -3, 1, -1), (6, -6, 2, -2, 4, -4), (5, -5, 7, -7, 8))
 RING = {0: 0, 1: 1, 2: 2, 3: 1}
 PLANE = sorted(
     ((dx, dy) for dx in range(4) for dy in range(4) if dx or dy), key=lambda p: -RING[p[0]] - RING[p[1]]
@@ -270,7 +270,10 @@
     for k in range(K):
         for l in range(K):
             inner(16 + 4 * k + l, x[k], res[l])
-            inner(32 + 4 * k + l, res[k], res[l])
+            if k <= l:
+                both = jnp.sum(res[k] * res[l], axis=0, keepdims=True)
+                gather[32 + 4 * k + l : 33 + 4 * k + l, :] = both
+                gather[32 + 4 * l + k : 33 + 4 * l + k, :] = both
     here = dot(jnp.ones((8, TILE), F32), gather[...], trans_b=True)
 
     msg[0] = here[0:1]

time: 52.2 us -> 52 us (level)
  no operation moved by 1% of the time
where the time goes in v6:
time: 52 us; the launch traced here: 51.8 us
  Pallas kernels  50.6 us (97%)
  between operations  1.29 us (2%)
    pallas_call x1, Pallas kernels, step(): pl.pallas_call(body, out_shape=(pltpu.VMEM((BLOCKS, K, TILE), F32), pltpu...  49.9 us

profile of v6, /device:TPU:1, one launch (start us, length us, event | category | flops | bytes accessed | tf_op | source)
XLA Modules:
  0.0 51.8 jit_solution(2237394409621583529)
XLA Ops:
  1.3 49.9 %lanczos.1 = (f32[16,4,128]{2,1,0:T(4,128)S(1)}, f32[4,4]{1,0:T(4,128)S(1)}, f32[4,4]{1,0:T(4,128)S(1)}) custom-call(s32[1]{0:T(128)S(6)} %copy.11.count, s32[8]{0:T(128)} %rows_hbm.1, s32[8]{0:T(128)} %cols_hbm.1, f32[4,4]{1,0:T(4,128)} %coupling_hbm.1, f32[8,128,128]{2,1,0:T(8,128)} %tiles_hbm.1, f32[16,128]{1,0:T(8,128)} %bitcast.12, ...), custom_call_target="tpu_custom_call" | custom-call | tf_op jit(solution)/shard_map/lanczos/pallas_call | solution.py:388
  51.2 0.6 %hand_over.1 = (f32[16,4,128]{2,1,0:T(4,128)}, f32[4,4]{1,0:T(4,128)}, f32[4,4]{1,0:T(4,128)}) custom-call(f32[16,4,128]{2,1,0:T(4,128)S(1)} %get-tuple-element.9.refs_0_, f32[4,4]{1,0:T(4,128)S(1)} %get-tuple-element.10.refs_1_, f32[4,4]{1,0:T(4,128)S(1)} %get-tuple-element.11.refs_2_), custom_call_target="tpu_custom_call" | custom-call | tf_op jit(solution)/shard_map/hand_over/pallas_call | solution.py:428

commit v7 on v6

--- a/solution.py
+++ b/solution.py
@@ -74,21 +74,15 @@
     return p, ((ah * bh - p) + ah * bl + al * bh) + al * bl
 
 
-def fold_rows(x, e):
-    for s in (4, 2, 1):
-        x, r = two_sum(x, pltpu.roll(x, s, 0))
-        e = e + pltpu.roll(e, s, 0) + r
-    return x, e
-
-
 def sum_pairs(rows):
-    x, e = rows[0:8], jnp.zeros((8, TILE), F32)
-    for r in range(8, rows.shape[0], 8):
-        x, t = two_sum(x, rows[r : r + 8])
-        e = e + t
-    x, e = fold_rows(x, e)
-    lane = lax.broadcasted_iota(jnp.int32, (8, TILE), 1)
-    return x + jnp.where(lane >= 64, pltpu.roll(e, 64, 1), 0.0)
+    rows = [(jnp.broadcast_to(r, (8, TILE)), 0.0) for r in rows]
+    while len(rows) > 1:
+        pairs = []
+        for (x, e), (y, f) in zip(rows[::2], rows[1::2]):
+            x, r = two_sum(x, y)
+            pairs.append((x, e + f + r))
+        rows = pairs
+    return rows[0]
 
 
 def pick(row, base, stride_m, stride_k, stride_l):
@@ -108,7 +102,7 @@
 
 def body(count, rows_hbm, cols_hbm, coupling_hbm, tiles_hbm, energy_hbm, basis_hbm, prev_hbm,
          next_ref, alpha_ref, beta_ref,
-         rows, cols, coupling, xcol, xrow, tiles, parts, flipped, energy, prev, fsend, fbuf, dsend, dbuf, gather, red1, red2, msg,
+         rows, cols, coupling, xcol, xrow, tiles, parts, flipped, energy, prev, fbuf, dbuf, gather, red1, red2, msg,
          local, sent, xr, hr, pr, fr, gr, dr, ar1, ar2):
     i, j = lax.axis_index("row"), lax.axis_index("col")
     sib = (i + 1 - 2 * lax.rem(i, 2), j)
@@ -205,8 +199,7 @@
         v = xrow[r + lax.shift_right_logical(r, 4)]
         y = product(v, parts[t])
         for k in range(K):
-            fsend[k, t : t + 1, :] = y[k : k + 1, :]
-    fbuf[i] = fsend[...]
+            fbuf[i, k, t : t + 1, :] = y[k : k + 1, :]
     onward(fbuf, 2, fr, gr, 0)
 
     arrive(xcol, 0, xr, hr, WAVES[1])
@@ -219,8 +212,7 @@
         v = xcol[r + lax.shift_right_logical(r, 4)]
         y = product(v, flipped[t])
         for k in range(K):
-            dsend[k, t : t + 1, :] = y[k : k + 1, :]
-    dbuf[j] = dsend[...]
+            dbuf[j, k, t : t + 1, :] = y[k : k + 1, :]
     over_plane(dbuf.at[j], dbuf.at[j], 5, dr)
     arrive(fbuf, 2, fr, gr, LIST_WAVES[1])
 
@@ -281,7 +273,9 @@
 
     over_plane(msg.at[0], red1.at[j], 6, ar1)
     arrived(red1.at[pl.ds(0, COLS - 1)], ar1.at[0])
-    part = sum_pairs(red1[...].reshape(COLS, TILE))
+    part, lost = sum_pairs([red1[n] for n in range(COLS)])
+    lane = lax.broadcasted_iota(jnp.int32, (8, TILE), 1)
+    part = part + jnp.where(lane >= 64, pltpu.roll(lost, 64, 1), 0.0)
     msg[1] = part[0:1]
     red2[i] = part[0:1]
 
@@ -291,13 +285,20 @@
     copy(msg.at[1], red2.at[i], sent.at[7], ar2.at[0], sib).start()
     arrived(red2.at[pl.ds(0, ROWS - 1)], ar2.at[0])
 
-    sums = sum_pairs(red2[...].reshape(ROWS, TILE)) * (1.0 / TOTAL)
-
-    g_km, g_km_low = pick(sums, 0, 1, 4, 0), pick(sums, 64, 1, 4, 0)
+    sums, lost = sum_pairs([red2[n] for n in range(ROWS)])
+    sums, lost = sums * (1.0 / TOTAL), lost * (1.0 / TOTAL)
+
+    def pick_low(base, *strides):
+        return [a + b for a, b in zip(pick(sums, 64 + base, *strides), pick(lost, base, *strides))]
+
+    def moved(base):
+        low = pltpu.roll(sums, TILE - 64 - base, 1) + pltpu.roll(lost, TILE - base, 1)
+        return pltpu.roll(sums, TILE - base, 1), low
+
+    g_km, g_km_low = pick(sums, 0, 1, 4, 0), pick_low(0, 1, 4, 0)
     f_ml = pick(sums, 16, 4, 0, 1)
-    f_mk, f_mk_low = pick(sums, 16, 4, 1, 0), pick(sums, 80, 4, 1, 0)
-    first, first_low = pltpu.roll(sums, TILE - 16, 1), pltpu.roll(sums, TILE - 80, 1)
-    resid, resid_low = pltpu.roll(sums, TILE - 32, 1), pltpu.roll(sums, TILE - 96, 1)
+    f_mk, f_mk_low = pick(sums, 16, 4, 1, 0), pick_low(16, 4, 1, 0)
+    (first, first_low), (resid, resid_low) = moved(16), moved(32)
     gf = (g_km[0] * f_ml[0] + g_km[1] * f_ml[1]) + (g_km[2] * f_ml[2] + g_km[3] * f_ml[3])
     alpha = first + (first - gf)
     a_ml, a_mk = pick(alpha, 0, 4, 0, 1), pick(alpha, 0, 4, 1, 0)
@@ -405,9 +406,7 @@
             pltpu.VMEM((SLOTS, 3 * TILE, TILE), jnp.bfloat16),
             pltpu.VMEM((BLOCKS, TILE), F32),
             pltpu.VMEM((BLOCKS, K, TILE), F32),
-            pltpu.VMEM((K, SLOTS, TILE), F32),
             pltpu.VMEM((ROWS, K, SLOTS, TILE), F32),
-            pltpu.VMEM((K, SLOTS, TILE), F32),
             pltpu.VMEM((COLS, K, SLOTS, TILE), F32),
             pltpu.VMEM((TILE, TILE), F32),
             pltpu.VMEM((COLS, 1, TILE), F32),

time: 52 us -> 51.9 us (level)
  no operation moved by 1% of the time
where the time goes in v7:
time: 51.9 us; the launch traced here: 51.7 us
  Pallas kernels  50.4 us (97%)
  between operations  1.29 us (2%)
    pallas_call x1, Pallas kernels, step(): pl.pallas_call(body, out_shape=(pltpu.VMEM((BLOCKS, K, TILE), F32), pltpu...  49.8 us

profile of v7, /device:TPU:1, one launch (start us, length us, event | category | flops | bytes accessed | tf_op | source)
XLA Modules:
  0.0 51.7 jit_solution(7985369669500954319)
XLA Ops:
  1.3 49.8 %lanczos.1 = (f32[16,4,128]{2,1,0:T(4,128)S(1)}, f32[4,4]{1,0:T(4,128)S(1)}, f32[4,4]{1,0:T(4,128)S(1)}) custom-call(s32[1]{0:T(128)S(6)} %copy.11.count, s32[8]{0:T(128)} %rows_hbm.1, s32[8]{0:T(128)} %cols_hbm.1, f32[4,4]{1,0:T(4,128)} %coupling_hbm.1, f32[8,128,128]{2,1,0:T(8,128)} %tiles_hbm.1, f32[16,128]{1,0:T(8,128)} %bitcast.12, ...), custom_call_target="tpu_custom_call" | custom-call | tf_op jit(solution)/shard_map/lanczos/pallas_call | solution.py:389
  51.1 0.6 %hand_over.1 = (f32[16,4,128]{2,1,0:T(4,128)}, f32[4,4]{1,0:T(4,128)}, f32[4,4]{1,0:T(4,128)}) custom-call(f32[16,4,128]{2,1,0:T(4,128)S(1)} %get-tuple-element.9.refs_0_, f32[4,4]{1,0:T(4,128)S(1)} %get-tuple-element.10.refs_1_, f32[4,4]{1,0:T(4,128)S(1)} %get-tuple-element.11.refs_2_), custom_call_target="tpu_custom_call" | custom-call | tf_op jit(solution)/shard_map/hand_over/pallas_call | solution.py:427
